TPU v7x, 32 devices: a whole 2x2x4 slice. The times are simulated.
32 devices in a mesh: gx: 8 (over z, y), gy: 4 (over x, core).
Axes of the slice: x: 2, y: 2, z: 4, core: 2. Of those that a mesh axis runs over, the one named last changes fastest.
Arguments:
- fields: float32 [4, 8, 1024, 512], P(None, None, 'gx', 'gy'), may hold values from -6 to 6
- shift_x: float32 [8, 1024, 512], P(None, 'gx', 'gy'), may hold values from -0.5 to 0.5
- shift_y: float32 [8, 1024, 512], P(None, 'gx', 'gy'), may hold values from -0.5 to 0.5
- block_offset: int32 [64, 4], P(None, 'gy'), may hold values from -23 to 23, as said below
- group_inverse: float32 [8, 1024, 128], P(None, 'gx'), as said below
- lower_coupling: float32 [8, 8], P(None, 'gx'), as said below
- upper_coupling: float32 [8, 8], P(None, 'gx'), as said below
Outputs:
- wind_fields: float32 [2, 8, 1024, 512], P(None, None, 'gx', 'gy')
- tracers: float32 [2, 8, 1024, 512], P(None, None, 'gx', 'gy')
Inputs may be any that keep to these rules, and one draw needn't show every extreme that they name: `block_offset`: within each aligned run of 8 x-blocks (the blocks of 128 consecutive columns at one y-block), every block departs from a block in the same run or in one of the two runs before or after it, and that run lies inside the grid; at most 4 blocks of a run depart from any one run, and exactly 4 depart from a run two runs away. `group_inverse`: entries are positive. `lower_coupling`: Negative. `upper_coupling`: Negative.
All inputs are finite; a program needn't handle non-finite values.
Results may differ from a plain program's by a relative error of at most 0.0003.
Values sent between devices are 32-bit elements; how exact they have to be, the bound alone decides.
A program may use at most 128 MiB of HBM per device.

v0:
```python
import jax
import jax.numpy as jnp
from jax import lax
from jax.sharding import PartitionSpec as P

BX = 16


PRECISE = lax.Precision.HIGHEST


def padded_2(block, sides, width):
    for axis, dim in sides:
        count = lax.axis_size(axis)
        forward = [(i, i + 1) for i in range(count - 1)]
        backward = [(target, source) for source, target in forward]
        low = lax.ppermute(
            lax.slice_in_dim(block, block.shape[dim] - width, None, axis=dim), axis, forward
        )
        high = lax.ppermute(lax.slice_in_dim(block, 0, width, axis=dim), axis, backward)
        block = jnp.concatenate([low, block, high], axis=dim)
    return block


def shifted_2(value, axis, steps):
    count = lax.axis_size(axis)
    leading, last = (max(0, -steps), min(count, count - steps))
    return lax.ppermute(value, axis, [(source, source + steps) for source in range(leading, last)])


def carried_in(value, axis, combine, identity, reverse):
    length, position = (lax.axis_size(axis), lax.axis_index(axis))
    everything = jax.tree.map(lambda part: lax.all_gather(part, axis), value)
    start = jax.tree.map(
        lambda part, zero: jnp.broadcast_to(jnp.asarray(zero, part.dtype), part.shape),
        value,
        identity,
    )

    def hop(k, before):
        at = length - 1 - k if reverse else k
        reached = at > position if reverse else at < position
        new = combine(before, jax.tree.map(lambda part: part[at], everything))
        return jax.tree.map(lambda a, b: jnp.where(reached, a, b), new, before)

    return lax.fori_loop(0, length, hop, start)


def lagrange(displace):
    position = -displace
    weights = []
    for target in range(-2, 3):
        factor = jnp.ones_like(position)
        for anchor in range(-2, 3):
            if anchor != target:
                factor = factor * ((position - anchor) / (target - anchor))
        weights.append(factor)
    return weights


def interpolate(window, across, along, span_x, span_y):
    weights_x = lagrange(across)
    weights_y = lagrange(along)
    running_total = None
    for column_tap in range(5):
        partial_sum = weights_y[0] * window[..., column_tap : column_tap + span_x, 0:span_y]
        for row_tap in range(1, 5):
            partial_sum = (
                partial_sum
                + weights_y[row_tap]
                * window[..., column_tap : column_tap + span_x, row_tap : row_tap + span_y]
            )
        tap_term = weights_x[column_tap] * partial_sum
        running_total = tap_term if running_total is None else running_total + tap_term
    return running_total


def compose(earlier, latter):
    product = jnp.einsum("...ij,...jk->...ik", latter, earlier, precision=PRECISE)
    return product / product[..., 1:2, 1:2]


def chain_affine(earlier, latter):
    return (latter[0] * earlier[0], latter[0][..., None, :, None] * earlier[1] + latter[1])


def mobius(lead_left, tail_left, lead_right, tail_right):
    upper_row = jnp.stack([tail_left * lead_right - tail_right * lead_left, tail_right], axis=-1)
    lower_row = jnp.stack([-lead_left, jnp.ones_like(lead_left)], axis=-1)
    return jnp.stack([upper_row, lower_row], axis=-2)


def local(fields, shift_x, shift_y, block_offset, group_inverse, lower_coupling, upper_coupling):
    field_count, level_count, columns, rows_here = fields.shape
    block_count = columns // BX
    position = lax.axis_index("gx")
    padded = padded_2(fields, (("gx", 2), ("gy", 3)), 2)
    offsets = block_offset[:, 0]
    inside = jnp.arange(block_count, dtype=jnp.int32)
    own_offset = lax.dynamic_slice_in_dim(offsets, position * block_count, block_count)
    shifted = []
    for step_distance in (2, 1, -1, -2):
        shifted.append(shifted_2(padded, "gx", step_distance))
    window_field = jnp.concatenate(
        [
            shifted[0][:, :, 0 : columns + 2],
            shifted[1][:, :, 2 : columns + 2],
            padded[:, :, 2 : columns + 2],
            shifted[2][:, :, 2 : columns + 2],
            shifted[3][:, :, 2 : columns + 4],
        ],
        axis=2,
    )
    starts = (inside - own_offset) * BX + 2 * columns
    windows = jnp.stack(
        [
            lax.dynamic_slice_in_dim(window_field, starts[column_block], BX + 4, 2)
            for column_block in range(block_count)
        ]
    )
    across = shift_x.reshape(level_count, block_count, BX, rows_here).transpose(1, 0, 2, 3)[:, None]
    along = shift_y.reshape(level_count, block_count, BX, rows_here).transpose(1, 0, 2, 3)[:, None]
    interpolated = interpolate(windows, across, along, BX, rows_here)
    advected = interpolated.transpose(1, 2, 0, 3, 4).reshape(
        field_count, level_count, columns, rows_here
    )
    local_solve = jnp.einsum("lij,wljy->wliy", group_inverse, advected[0:2], precision=PRECISE)
    lower_here = lower_coupling[:, 0]
    upper_here = upper_coupling[:, 0]
    left_spike = group_inverse[:, :, 0] * lower_here[:, None]
    right_spike = group_inverse[:, :, columns - 1] * upper_here[:, None]
    lead_left = left_spike[:, 0]
    tail_left = left_spike[:, columns - 1]
    lead_right = right_spike[:, 0]
    tail_right = right_spike[:, columns - 1]
    first_row = local_solve[:, :, 0, :]
    last_row = local_solve[:, :, columns - 1, :]
    identity_map = jnp.broadcast_to(jnp.eye(2, dtype=jnp.float32), (level_count, 2, 2))
    ones_level = jnp.ones((level_count,), jnp.float32)
    zeros_rows = jnp.zeros_like(first_row)
    before = carried_in(
        mobius(lead_left, tail_left, lead_right, tail_right), "gx", compose, identity_map, False
    )
    gain_here = before[:, 0, 1] / before[:, 1, 1]
    pivot_here = 1.0 - lead_left * gain_here
    ratio_here = tail_left * gain_here / pivot_here
    forward_map = (
        -(ratio_here * lead_left + tail_left),
        ratio_here[None, :, None] * first_row + last_row,
    )
    behind = carried_in(forward_map, "gx", chain_affine, (ones_level, zeros_rows), False)[1]
    lead_value = first_row - lead_left[None, :, None] * behind
    backward_map = (-lead_right / pivot_here, lead_value / pivot_here[None, :, None])
    ahead_value = carried_in(backward_map, "gx", chain_affine, (ones_level, zeros_rows), True)[1]
    first_value = backward_map[1] + backward_map[0][None, :, None] * ahead_value
    left_value = behind - gain_here[None, :, None] * first_value
    wind_fields = (
        local_solve
        - left_spike[None, :, :, None] * left_value[:, :, None, :]
        - right_spike[None, :, :, None] * ahead_value[:, :, None, :]
    )
    return (wind_fields, advected[2:4])


def solution(mesh):
    return jax.shard_map(
        local,
        mesh=mesh,
        in_specs=(
            P(None, None, "gx", "gy"),
            P(None, "gx", "gy"),
            P(None, "gx", "gy"),
            P(None, "gy"),
            P(None, "gx", None),
            P(None, "gx"),
            P(None, "gx"),
        ),
        out_specs=(P(None, None, "gx", "gy"), P(None, None, "gx", "gy")),
        check_vma=False,
    )
```

profile of v0, /device:TPU:0, one launch (start us, length us, event | category | flops | bytes accessed | tf_op | source)
XLA Modules:
  0.0 575.3 jit_solution(1927487869277992607)
XLA Ops:
  1.7 4.9 collective-permute-start
  10.3 2.8 constant_dynamic-update-slice_fusion.1
  13.1 2.7 fusion.66
  15.8 2.8 copy.98
  19.9 2.8 copy.97
  22.7 3.0 collective-permute-start.2
  25.9 32.9 %all-gather = f32[64,2,2]{2,1,0:T(2,128)S(1)} all-gather(f32[8,2,2]{2,1,0:T(2,128)S(1)} %copy.109), channel_id=2, replica_groups=mesh['gx'=8,'gy'=4] {'gx'}, dimensions={0}, use_global_device_ids=true | all-gather | bytes 1152 | tf_op jit(solution)/shard_map/all_gather | solution.py:33
  58.9 2.6 copy.100
  61.5 2.6 copy.99
  64.1 6.0 %pad_maximum_fusion = f32[4,8,132,132]{3,1,2,0:T(8,128)} fusion(f32[4,8,132,2]{3,1,2,0:T(8,128)} %copy.100, f32[4,8,132,128]{3,1,2,0:T(8,128)S(1)} %constant_dynamic-update-slice_fusion, f32[4,8,132,2]{3,1,2,0:T(8,128)} %copy.99), kind=kLoop, calls=%fused_computation.9 | loop fusion | flops 1115136 | bytes 4460544 | tf_op jit(solution)/shard_map/concatenate | solution.py:21
  70.2 3.5 collective-permute-start.4
  73.7 4.6 collective-permute-start.5
  78.2 5.0 while.43
  101.1 163.7 %all-gather.2 = f32[8,1,8]{2,1,0:T(1,128)S(1)} all-gather(f32[1,1,8]{2,1,0:T(1,128)S(1)} %get-tuple-element.460), channel_id=1, replica_groups=mesh['gx'=8,'gy'=4] {'gx'}, dimensions={0}, use_global_device_ids=true | all-gather | bytes 288 | tf_op jit(solution)/shard_map/all_gather | solution.py:33
  264.8 19.4 %all-gather.3 = f32[8,1,8]{2,1,0:T(1,128)S(1)} all-gather(f32[1,1,8]{2,1,0:T(1,128)S(1)} %get-tuple-element.461), channel_id=1, replica_groups=mesh['gx'=8,'gy'=4] {'gx'}, dimensions={0}, use_global_device_ids=true | all-gather | bytes 288 | tf_op jit(solution)/shard_map/all_gather | solution.py:33
  287.0 4.2 fusion.36
  291.1 2.6 slice_dynamic-update-slice_fusion.1
  293.8 2.8 slice_dynamic-update-slice_fusion.4
  296.6 2.8 slice_dynamic-update-slice_fusion.3
  299.4 70.4 %collective-permute-done.6 = f32[4,8,132,132]{3,1,2,0:T(8,128)S(1)} collective-permute-done((f32[4,8,132,132]{3,1,2,0:T(8,128)}, f32[4,8,132,132]{3,1,2,0:T(8,128)S(1)}, u32[]{:S(2)}, u32[]{:S(2)}) %collective-permute-start.6) | collective-permute-done | bytes 2230304 | tf_op jit(solution)/shard_map/ppermute | solution.py:28
  370.5 90.2 %collective-permute-done.7 = f32[4,8,132,132]{3,1,2,0:T(8,128)S(1)} collective-permute-done((f32[4,8,132,132]{3,1,2,0:T(8,128)}, f32[4,8,132,132]{3,1,2,0:T(8,128)S(1)}, u32[]{:S(2)}, u32[]{:S(2)}) %collective-permute-start.7) | collective-permute-done | bytes 2230304 | tf_op jit(solution)/shard_map/ppermute | solution.py:28
  468.6 38.2 %fusion.5 = f32[4,8,8,16,128]{4,1,3,0,2:T(8,128)S(1)} fusion(f32[8,4,8,20,132]{4,2,3,1,0:T(8,128)} %bitcast_dynamic-update-slice_fusion, f32[8,8,16,128]{3,1,2,0:T(8,128)} %get-tuple-element.475, f32[8,8,16,128]{3,1,2,0:T(8,128)} %get-tuple-element.474, f32[8,8,16,128]{3,1,2,0:T(8,128)} %get-tuple-element.472, f32[8,8,16,128]{3,1,2,0:T(8,128)} %get-tuple-element.473, ...), kind=kLoop, calls=%fused_computation.19 | loop fusion | flops 28311552 | bytes 59768832 | tf_op jit(solution)/shard_map/transpose | solution.py:124
  509.7 30.5 %all_gather.27 = f32[8,2,8,128]{3,2,1,0:T(8,128)S(1)} all-gather(f32[1,2,8,128]{3,2,1,0:T(8,128)S(1)} %fusion.52), channel_id=1, replica_groups=mesh['gx'=8,'gy'=4] {'gx'}, dimensions={0}, use_global_device_ids=true | all-gather | bytes 73728 | tf_op jit(solution)/shard_map/all_gather | solution.py:33
  540.9 30.5 %all-gather.1 = f32[16,8,128]{2,1,0:T(8,128)S(1)} all-gather(f32[2,8,128]{2,1,0:T(8,128)S(1)} %fusion.53), channel_id=3, replica_groups=mesh['gx'=8,'gy'=4] {'gx'}, dimensions={0}, use_global_device_ids=true | all-gather | bytes 73728 | tf_op jit(solution)/shard_map/all_gather | solution.py:33
  (148 shorter events, 34.0 us)
Async XLA Ops:
  0.6 9.0 %copy-start.4 = (f32[8,1]{0,1:T(1,128)S(1)}, f32[8,1]{0,1:T(1,128)}, u32[]{:S(2)}) copy-start(f32[8,1]{0,1:T(1,128)} %param.18) | copy-start | bytes 100
  0.6 9.0 %copy-start.3 = (f32[8,1]{0,1:T(1,128)S(1)}, f32[8,1]{0,1:T(1,128)}, u32[]{:S(2)}) copy-start(f32[8,1]{0,1:T(1,128)} %param.19) | copy-start | bytes 100
  1.7 8.6 %collective-permute-start = (f32[4,8,2,128]{3,1,2,0:T(8,128)S(1)}, f32[4,8,2,128]{3,1,2,0:T(8,128)S(1)}, u32[]{:S(2)}, u32[]{:S(2)}) collective-permute-start(f32[4,8,2,128]{3,1,2,0:T(8,128)S(1)} %copy.132), channel_id=1, source_target_pairs={{0,4},{4,8},{8,12},{12,16},{16,20},{20,24},{24,28},{1,5},{5,9},{9,... | collective-permute-start | bytes 98312 | tf_op jit(solution)/shard_map/ppermute | solution.py:17
  6.6 6.5 %collective-permute-start.1 = (f32[4,8,2,128]{3,1,2,0:T(8,128)S(1)}, f32[4,8,2,128]{3,1,2,0:T(8,128)S(1)}, u32[]{:S(2)}, u32[]{:S(2)}) collective-permute-start(f32[4,8,2,128]{3,1,2,0:T(8,128)S(1)} %copy.133), channel_id=1, source_target_pairs={{4,0},{8,4},{12,8},{16,12},{20,16},{24,20},{28,24},{5,1},{9,5},{13... | collective-permute-start | bytes 98312 | tf_op jit(solution)/shard_map/ppermute | solution.py:20
  18.6 40.3 %collective-permute-start.3 = (f32[4,8,132,2]{2,1,3,0:T(8,128)S(1)}, f32[4,8,132,2]{2,1,3,0:T(8,128)S(1)}, u32[]{:S(2)}, u32[]{:S(2)}) collective-permute-start(f32[4,8,132,2]{2,1,3,0:T(8,128)S(1)} %copy.98), channel_id=1, source_target_pairs={{1,0},{2,1},{3,2},{5,4},{6,5},{7,6},{9,8},{10,9},{11,10},{13,12},{... | collective-permute-start | bytes 101384 | tf_op jit(solution)/shard_map/ppermute | solution.py:20
  22.7 38.8 %collective-permute-start.2 = (f32[4,8,132,2]{2,1,3,0:T(8,128)S(1)}, f32[4,8,132,2]{2,1,3,0:T(8,128)S(1)}, u32[]{:S(2)}, u32[]{:S(2)}) collective-permute-start(f32[4,8,132,2]{2,1,3,0:T(8,128)S(1)} %copy.97), channel_id=1, source_target_pairs={{0,1},{1,2},{2,3},{4,5},{5,6},{6,7},{8,9},{9,10},{10,11},{12,13},{... | collective-permute-start | bytes 101384 | tf_op jit(solution)/shard_map/ppermute | solution.py:17
  64.1 19.1 %copy-start.5 = (s32[64,1]{0,1:T(1,128)S(1)}, s32[64,1]{0,1:T(1,128)}, u32[]{:S(2)}) copy-start(s32[64,1]{0,1:T(1,128)} %param.16) | copy-start | bytes 772
  64.1 30.1 %copy-start.1 = (f32[8,128,128]{2,1,0:T(8,128)S(1)}, f32[8,128,128]{2,1,0:T(8,128)}, u32[]{:S(2)}) copy-start(f32[8,128,128]{2,1,0:T(8,128)} %param.14) | copy-start | bytes 1572868
  70.2 24.9 %copy-start.2 = (f32[8,128,128]{2,1,0:T(8,128)S(1)}, f32[8,128,128]{2,1,0:T(8,128)}, u32[]{:S(2)}) copy-start(f32[8,128,128]{2,1,0:T(8,128)} %param.15) | copy-start | bytes 1572868
  70.2 221.0 %collective-permute-start.4 = (f32[4,8,132,132]{3,1,2,0:T(8,128)}, f32[4,8,132,132]{3,1,2,0:T(8,128)}, u32[]{:S(2)}, u32[]{:S(2)}) collective-permute-start(f32[4,8,132,132]{3,1,2,0:T(8,128)} %pad_maximum_fusion), channel_id=1, source_target_pairs={{0,8},{4,12},{8,16},{12,20},{16,24},{20,28},{1,9},{5,13},{9,17},{1... | collective-permute-start | bytes 6690824 | tf_op jit(solution)/shard_map/ppermute | solution.py:28
  73.7 220.1 %collective-permute-start.5 = (f32[4,8,132,132]{3,1,2,0:T(8,128)}, f32[4,8,132,132]{3,1,2,0:T(8,128)}, u32[]{:S(2)}, u32[]{:S(2)}) collective-permute-start(f32[4,8,132,132]{3,1,2,0:T(8,128)} %pad_maximum_fusion), channel_id=1, source_target_pairs={{0,4},{4,8},{8,12},{12,16},{16,20},{20,24},{24,28},{1,5},{5,9},{9,... | collective-permute-start | bytes 6690824 | tf_op jit(solution)/shard_map/ppermute | solution.py:28
  284.2 85.7 %collective-permute-start.6 = (f32[4,8,132,132]{3,1,2,0:T(8,128)}, f32[4,8,132,132]{3,1,2,0:T(8,128)S(1)}, u32[]{:S(2)}, u32[]{:S(2)}) collective-permute-start(f32[4,8,132,132]{3,1,2,0:T(8,128)} %pad_maximum_fusion), channel_id=1, source_target_pairs={{4,0},{8,4},{12,8},{16,12},{20,16},{24,20},{28,24},{5,1},{9,5},{13... | collective-permute-start | bytes 6690824 | tf_op jit(solution)/shard_map/ppermute | solution.py:28
  285.5 175.2 %collective-permute-start.7 = (f32[4,8,132,132]{3,1,2,0:T(8,128)}, f32[4,8,132,132]{3,1,2,0:T(8,128)S(1)}, u32[]{:S(2)}, u32[]{:S(2)}) collective-permute-start(f32[4,8,132,132]{3,1,2,0:T(8,128)} %pad_maximum_fusion), channel_id=1, source_target_pairs={{8,0},{12,4},{16,8},{20,12},{24,16},{28,20},{9,1},{13,5},{17,9},{2... | collective-permute-start | bytes 6690824 | tf_op jit(solution)/shard_map/ppermute | solution.py:28
  506.9 1.0 copy-start
where the time goes:
time: 576 us; the launch traced here: 575 us
  blocking collectives  277 us (48%)
  waiting for transfers between devices  161 us (28%)
  other arithmetic  53.6 us (9%)
  local copies, waits for them, and re-layouts  44.2 us (8%)
  starting transfers between devices  21.3 us (4%)
  between operations  15.9 us (3%)
    all_gather x5, blocking collectives, carried_in(): everything = jax.tree.map(lambda part: lax.all_gather(part, axis), value)  277 us
    ppermute x4, waiting for transfers between devices, shifted_2(): lax.ppermute(value, axis, [(source, source + steps) for source in range(l...  161 us
    transpose x1, other arithmetic, local(): interpolated.transpose(1, 2, 0, 3, 4)  38.2 us
    unnamed x31, local copies, waits for them, and re-layouts  20.6 us
  transfers between devices with their start and end apart: 8, of which 2 were waited for; matrix products, arithmetic and copies ran while one was open for 5% of the time, Pallas kernels for 0%

commit v1 on v0

v1 whole, which is shorter than its diff:
```python
import functools

import jax
import jax.numpy as jnp
from jax import lax
from jax.experimental import pallas as pl
from jax.experimental.pallas import tpu as pltpu
from jax.sharding import PartitionSpec as P

BX = 16
CAP = 4
DELTA = (2, -2, 1, -1)
REMOTE = CAP * len(DELTA)
SLOTS = REMOTE + CAP
ROWS = BX + 5
MESH = pl.DeviceIdType.MESH


def weights_of(shift):
    p = -shift
    a, b, c, d = p + 2.0, p + 1.0, p - 1.0, p - 2.0
    ab, cd = a * b, c * d
    pcd, pab = p * cd, p * ab
    return (
        b * pcd * (1.0 / 24.0),
        a * pcd * (-1.0 / 6.0),
        ab * cd * 0.25,
        pab * d * (-1.0 / 6.0),
        pab * c * (1.0 / 24.0),
    )


def kernel(
    n, m, nb,
    offs, xm, shx, shy, ginv, low, upp,
    wind, tracers,
    side_rows, edge, edge_lo, edge_hi, rims, send, recv, adv, wgt, solved, spikes, coef, iface, work,
    ilist, blist,
    halo_s, halo_r, slot_s, slot_r, rim_s, rim_r, coef_s, coef_r, if_s, if_r,
):
    levels, cols, lanes = 8, nb * BX, 128
    s, r = lax.axis_index("gx"), lax.axis_index("gy")
    lane = lax.broadcasted_iota(jnp.int32, (8, lanes), 1)
    zero = jnp.zeros((8, lanes), jnp.float32)

    def valid(ds, dr):
        return (s + ds >= 0) & (s + ds < n) & (r + dr >= 0) & (r + dr < m)

    for f in range(4):
        for x in range(4):
            side_rows[x, f] = zero
        for b in range(nb + 2):
            edge_lo[b, f] = zero
            edge_hi[b, f] = zero

    barrier = pltpu.get_barrier_semaphore()
    diagonal = [(ds, dr) for ds in (-1, 0, 1) for dr in (-1, 1)]

    def greet(d, carry):
        @pl.when(d != s)
        def _():
            pl.semaphore_signal(barrier, inc=1, device_id=(d, r), device_id_type=MESH)
        return carry

    lax.fori_loop(0, n, greet, 0)
    for ds, dr in diagonal:
        @pl.when(valid(ds, dr))
        def _():
            pl.semaphore_signal(barrier, inc=1, device_id=(s + ds, r + dr), device_id_type=MESH)

    def edges(b, carry):
        for f in range(4):
            acc = zero
            for j in range(BX):
                at = 4 * (j + 2)
                moved = pltpu.roll(xm[b * BX + j, f], at, 1)
                acc = jnp.where((lane >= at - 2) & (lane < at + 2), moved, acc)
            edge[b, f] = acc
        return carry

    lax.fori_loop(0, nb, edges, 0)

    lower = jnp.broadcast_to(low[...], (8, lanes))
    upper = jnp.broadcast_to(upp[...], (8, lanes))
    first = jnp.concatenate([ginv[l * cols:l * cols + 1, :] for l in range(levels)], axis=0)
    final = jnp.concatenate([ginv[(l + 1) * cols - 1:(l + 1) * cols, :] for l in range(levels)], axis=0)
    coef[s, 0] = jnp.broadcast_to(first[:, 0:1], (8, lanes)) * lower
    coef[s, 1] = jnp.broadcast_to(final[:, 0:1], (8, lanes)) * lower
    coef[s, 2] = jnp.broadcast_to(first[:, cols - 1:cols], (8, lanes)) * upper
    coef[s, 3] = jnp.broadcast_to(final[:, cols - 1:cols], (8, lanes)) * upper

    def listed(dest, source):
        base = jnp.clip(dest, 0, n - 1) * nb
        count = jnp.int32(0)
        picks = [(jnp.int32(0), jnp.int32(0)) for _ in range(CAP)]
        for i in range(nb):
            g = base + i - offs[base + i]
            hit = (g >= source * nb) & (g < source * nb + nb)
            for k in range(CAP):
                here = hit & (count == k)
                picks[k] = (
                    jnp.where(here, jnp.int32(i), picks[k][0]),
                    jnp.where(here, g - source * nb, picks[k][1]),
                )
            count = count + jnp.where(hit, 1, 0)
        return picks

    for e, delta in enumerate(DELTA):
        outgoing = listed(s + delta, s)
        incoming = listed(s, s - delta)
        for k in range(CAP):
            blist[k * 4 + e] = outgoing[k][1]
            ilist[k * 4 + e] = incoming[k][0]
    own = listed(s, s)
    for k in range(CAP):
        blist[REMOTE + k] = own[k][1]
        ilist[REMOTE + k] = own[k][0]

    pl.semaphore_wait(
        barrier, n - 1 + sum(jnp.where(valid(ds, dr), 1, 0) for ds, dr in diagonal)
    )

    halo = [
        (1, 0, xm.at[pl.ds(cols - 2, 2)], side_rows.at[pl.ds(0, 2)]),
        (-1, 0, xm.at[pl.ds(0, 2)], side_rows.at[pl.ds(2, 2)]),
        (0, 1, edge, edge_lo.at[pl.ds(1, nb)]),
        (0, -1, edge, edge_hi.at[pl.ds(1, nb)]),
        (1, 1, edge.at[nb - 1], edge_lo.at[0]),
        (1, -1, edge.at[nb - 1], edge_hi.at[0]),
        (-1, 1, edge.at[0], edge_lo.at[nb + 1]),
        (-1, -1, edge.at[0], edge_hi.at[nb + 1]),
    ]

    def halo_copy(q):
        ds, dr, source, target = halo[q]
        return pltpu.make_async_remote_copy(
            src_ref=source, dst_ref=target, send_sem=halo_s.at[q], recv_sem=halo_r.at[q],
            device_id=(s + ds, r + dr), device_id_type=MESH,
        )

    for q in range(8):
        @pl.when(valid(halo[q][0], halo[q][1]))
        def _(q=q):
            halo_copy(q).start()

    def share(buffer, sends, recvs, d):
        return pltpu.make_async_remote_copy(
            src_ref=buffer.at[s], dst_ref=buffer.at[s], send_sem=sends.at[d],
            recv_sem=recvs.at[s], device_id=(d, r), device_id_type=MESH,
        )

    def shared(buffer, sends, recvs, d):
        return pltpu.make_async_remote_copy(
            src_ref=buffer.at[d], dst_ref=buffer.at[d], send_sem=sends.at[d],
            recv_sem=recvs.at[d], device_id=(d, r), device_id_type=MESH,
        )

    def others(act):
        def step(d, carry):
            @pl.when(d != s)
            def _():
                act(d)
            return carry
        lax.fori_loop(0, n, step, 0)

    def part_copy(slot, e, lo, size, sends, recvs, index):
        return pltpu.make_async_remote_copy(
            src_ref=send.at[slot, pl.ds(lo, size)], dst_ref=recv.at[slot, pl.ds(lo, size)],
            send_sem=sends.at[index], recv_sem=recvs.at[index],
            device_id=(s + DELTA[e], r), device_id_type=MESH,
        )

    def centre(into, slot, b):
        def row(j, carry):
            for f in range(4):
                into[slot, j, f] = xm[b * BX + j, f]
            return carry
        lax.fori_loop(0, BX, row, 0, unroll=4)

    def rim(into, slot, b):
        for j in range(5):
            for f in range(4):
                into[slot, BX + j, f] = rims[b, j, f]

    for e, delta in enumerate(DELTA):
        @pl.when(valid(delta, 0))
        def _(e=e):
            centre(send, e, blist[e])
            part_copy(e, e, 0, BX, slot_s, slot_r, e).start()

    others(lambda d: share(coef, coef_s, coef_r, d).start())

    for q in range(8):
        @pl.when(valid(-halo[q][0], -halo[q][1]))
        def _(q=q):
            halo_copy(q).wait_recv()

    before = ((lane + 2) & 3) < 2

    def make_rims(b, carry):
        for f in range(4):
            mid = jnp.where(before, edge_lo[b + 1, f], edge_hi[b + 1, f])
            prev = jnp.where(before, edge_lo[b, f], edge_hi[b, f])
            after = jnp.where(before, edge_lo[b + 2, f], edge_hi[b + 2, f])
            mid = jnp.where((lane >= 126) | (lane < 6), pltpu.roll(prev, 64, 1), mid)
            rims[b, 4, f] = jnp.where((lane >= 70) & (lane < 78), pltpu.roll(after, 64, 1), mid)
        return carry

    lax.fori_loop(0, nb, make_rims, 0)

    for b in range(nb):
        for f in range(4):
            for j in range(2):
                rims[b, j, f] = xm[b * BX - 2 + j, f] if b else side_rows[j, f]
                rims[b, 2 + j, f] = xm[b * BX + BX + j, f] if b < nb - 1 else side_rows[2 + j, f]

    for e, delta in enumerate(DELTA):
        @pl.when(valid(delta, 0))
        def _(e=e):
            rim(send, e, blist[e])
            part_copy(e, e, BX, 5, rim_s, rim_r, e).start()

    for k in range(1, CAP):
        for e, delta in enumerate(DELTA):
            @pl.when(valid(delta, 0))
            def _(e=e, slot=k * 4 + e):
                centre(send, slot, blist[slot])
                rim(send, slot, blist[slot])
                part_copy(slot, e, 0, ROWS, slot_s, slot_r, slot).start()

    for l in range(levels):
        def spike(x, carry, l=l):
            g = ginv[pl.ds(l * cols + x * 8, 8), :]
            spikes[0, l, pl.ds(x * 8, 8), :] = (
                jnp.broadcast_to(g[:, 0:1], (8, lanes)) * jnp.broadcast_to(low[l:l + 1, :], (8, lanes))
            )
            spikes[1, l, pl.ds(x * 8, 8), :] = (
                jnp.broadcast_to(g[:, cols - 1:cols], (8, lanes))
                * jnp.broadcast_to(upp[l:l + 1, :], (8, lanes))
            )
            return carry
        lax.fori_loop(0, cols // 8, spike, 0)

    def advect(buffer, slot):
        i = ilist[slot]

        def weigh(j, carry):
            for q, w in enumerate(weights_of(shx[i * BX + j])):
                wgt[j, q] = w
            for q, w in enumerate(weights_of(shy[i * BX + j])):
                wgt[j, 5 + q] = w
            return carry

        lax.fori_loop(0, BX, weigh, 0, unroll=2)

        def field(f, carry):
            side = buffer[slot, BX + 4, f]
            rows = []
            for x in range(BX + 4):
                at = BX + x if x < 2 else (x - 2 if x < BX + 2 else x)
                mid = buffer[slot, at, f]
                rimmed = side if x == 0 else pltpu.roll(side, lanes - 4 * x, 1)
                rows.append((
                    pltpu.roll(jnp.where(lane >= 126, rimmed, mid), 2, 1),
                    pltpu.roll(jnp.where(lane >= 127, rimmed, mid), 1, 1),
                    mid,
                    pltpu.roll(jnp.where(lane < 1, rimmed, mid), lanes - 1, 1),
                    pltpu.roll(jnp.where(lane < 2, rimmed, mid), lanes - 2, 1),
                ))
                if x >= 4:
                    j = x - 4
                    wy = [wgt[j, 5 + q] for q in range(5)]
                    total = None
                    for a in range(5):
                        part = wy[0] * rows[j + a][0]
                        for q in range(1, 5):
                            part = part + wy[q] * rows[j + a][q]
                        part = wgt[j, a] * part
                        total = part if total is None else total + part
                    adv[slot, pl.ds(f * levels * BX + j, levels, stride=BX), :] = total
            return carry

        lax.fori_loop(0, 4, field, 0)

    def local_slot(k, carry):
        slot = REMOTE + k
        b = blist[slot]
        centre(recv, slot, b)
        rim(recv, slot, b)
        advect(recv, slot)
        return carry

    lax.fori_loop(0, CAP, local_slot, 0)

    others(lambda d: shared(coef, coef_s, coef_r, d).wait_recv())

    def pivot_step(d, gain):
        ll, tl, lr, tr = (coef[d, q] for q in range(4))
        inverse = 1.0 / (1.0 - ll * gain)
        ratio = tl * gain * inverse
        work[d, 0] = gain
        work[d, 1] = inverse
        work[d, 2] = ratio
        return tr + ratio * lr

    lax.fori_loop(0, n, pivot_step, zero)

    for k in range(CAP):
        for e, delta in enumerate(DELTA):
            @pl.when(valid(-delta, 0))
            def _(e=e, k=k, slot=k * 4 + e):
                if k == 0:
                    part_copy(slot, e, 0, BX, slot_s, slot_r, slot).wait_recv()
                    part_copy(slot, e, BX, 5, rim_s, rim_r, e).wait_recv()
                else:
                    part_copy(slot, e, 0, ROWS, slot_s, slot_r, slot).wait_recv()
        def remote_slot(e, carry, k=k):
            advect(recv, k * 4 + e)
            return carry
        lax.fori_loop(0, 4, remote_slot, 0)

    runs = []
    for i in range(nb):
        g = s * nb + i - offs[s * nb + i]
        runs.append(lax.shift_right_arithmetic(g, jnp.int32(nb.bit_length() - 1)))
    for i in range(nb):
        count = jnp.int32(0)
        for j in range(i):
            count = count + jnp.where(runs[j] == runs[i], 1, 0)
        count = jnp.minimum(count, CAP - 1)
        gap = s - runs[i]
        place = REMOTE + count
        for e, delta in enumerate(DELTA):
            place = jnp.where(gap == delta, count * 4 + e, place)

        def put(l, carry, i=i, place=place):
            for w in range(2):
                at = pl.multiple_of((w * levels + l) * BX, BX)
                solved[w, l, pl.ds(i * BX, BX), :] = adv[place, pl.ds(at, BX), :]
                at = pl.multiple_of(((w + 2) * levels + l) * BX, BX)
                tracers[w, l, pl.ds(i * BX, BX), :] = adv[place, pl.ds(at, BX), :]
            return carry

        lax.fori_loop(0, levels, put, 0)

    def solve(l, carry):
        right = jnp.concatenate([solved[0, l], solved[1, l]], axis=1)
        g = ginv[pl.ds(pl.multiple_of(l * cols, cols), cols), :]
        out = jnp.dot(g, right, precision=lax.Precision.HIGHEST, preferred_element_type=jnp.float32)
        for w in range(2):
            part = out[:, w * lanes:(w + 1) * lanes]
            solved[w, l] = part
            iface[s, w, pl.ds(l, 1), :] = part[0:1]
            iface[s, 2 + w, pl.ds(l, 1), :] = part[cols - 1:cols]
        return carry

    lax.fori_loop(0, levels, solve, 0)

    others(lambda d: share(iface, if_s, if_r, d).start())
    others(lambda d: shared(iface, if_s, if_r, d).wait_recv())

    def forward(d, behind):
        ll, tl, ratio = coef[d, 0], coef[d, 1], work[d, 2]
        after = []
        for w in range(2):
            lead = iface[d, w] - ll * behind[w]
            work[d, 3 + w] = lead
            work[d, 5 + w] = behind[w]
            after.append(iface[d, 2 + w] - tl * behind[w] + ratio * lead)
        return tuple(after)

    lax.fori_loop(0, n, forward, (zero, zero))

    def backward(k, ahead):
        d = n - 1 - k
        lr, inverse = coef[d, 2], work[d, 1]
        values = []
        for w in range(2):
            work[d, 7 + w] = ahead[w]
            values.append((work[d, 3 + w] - lr * ahead[w]) * inverse)
            work[d, 9 + w] = values[w]
        return tuple(values)

    lax.fori_loop(0, n - s, backward, (zero, zero))

    for w in range(2):
        left = work[s, 5 + w] - work[s, 0] * work[s, 9 + w]
        ahead = work[s, 7 + w]
        for l in range(levels):
            here = left[l:l + 1]
            there = ahead[l:l + 1]
            wind[w, l] = solved[w, l] - spikes[0, l] * here - spikes[1, l] * there

    for q in range(8):
        @pl.when(valid(halo[q][0], halo[q][1]))
        def _(q=q):
            halo_copy(q).wait_send()
    others(lambda d: share(coef, coef_s, coef_r, d).wait_send())
    others(lambda d: share(iface, if_s, if_r, d).wait_send())
    for e, delta in enumerate(DELTA):
        @pl.when(valid(delta, 0))
        def _(e=e):
            part_copy(e, e, 0, BX, slot_s, slot_r, e).wait_send()
            part_copy(e, e, BX, 5, rim_s, rim_r, e).wait_send()
            for k in range(1, CAP):
                part_copy(k * 4 + e, e, 0, ROWS, slot_s, slot_r, k * 4 + e).wait_send()


def local(n, m, fields, shift_x, shift_y, block_offset, group_inverse, lower, upper):
    nf, levels, cols, lanes = fields.shape
    nb = cols // BX
    vmem = pl.BlockSpec(memory_space=pltpu.VMEM)
    f32 = jnp.float32
    tile = (8, lanes)
    dma = pltpu.SemaphoreType.DMA
    return pl.pallas_call(
        functools.partial(kernel, n, m, nb),
        out_shape=(
            jax.ShapeDtypeStruct((2, levels, cols, lanes), f32),
            jax.ShapeDtypeStruct((2, levels, cols, lanes), f32),
        ),
        in_specs=[pl.BlockSpec(memory_space=pltpu.SMEM)] + [vmem] * 6,
        out_specs=(vmem, vmem),
        scratch_shapes=[
            pltpu.VMEM((4, nf) + tile, f32),
            pltpu.VMEM((nb, nf) + tile, f32),
            pltpu.VMEM((nb + 2, nf) + tile, f32),
            pltpu.VMEM((nb + 2, nf) + tile, f32),
            pltpu.VMEM((nb, 5, nf) + tile, f32),
            pltpu.VMEM((REMOTE, ROWS, nf) + tile, f32),
            pltpu.VMEM((SLOTS, ROWS, nf) + tile, f32),
            pltpu.VMEM((SLOTS, (nf * levels + 1) * BX, lanes), f32),
            pltpu.VMEM((BX, 10) + tile, f32),
            pltpu.VMEM((2, levels, cols, lanes), f32),
            pltpu.VMEM((2, levels, cols, lanes), f32),
            pltpu.VMEM((n, 4) + tile, f32),
            pltpu.VMEM((n, 4) + tile, f32),
            pltpu.VMEM((n, 11) + tile, f32),
            pltpu.SMEM((SLOTS,), jnp.int32),
            pltpu.SMEM((SLOTS,), jnp.int32),
            dma((8,)), dma((8,)), dma((REMOTE,)), dma((REMOTE,)), dma((4,)), dma((4,)),
            dma((n,)), dma((n,)), dma((n,)), dma((n,)),
        ],
        compiler_params=pltpu.CompilerParams(
            collective_id=0, has_side_effects=True, vmem_limit_bytes=50 * 1024 * 1024
        ),
    )(
        block_offset[:, 0],
        fields.transpose(2, 0, 1, 3),
        shift_x.transpose(1, 0, 2),
        shift_y.transpose(1, 0, 2),
        group_inverse.reshape(-1, cols),
        lower,
        upper,
    )


def solution(mesh):
    return jax.shard_map(
        functools.partial(local, mesh.shape["gx"], mesh.shape["gy"]),
        mesh=mesh,
        in_specs=(
            P(None, None, "gx", "gy"),
            P(None, "gx", "gy"),
            P(None, "gx", "gy"),
            P(None, "gy"),
            P(None, "gx", None),
            P(None, "gx"),
            P(None, "gx"),
        ),
        out_specs=(P(None, None, "gx", "gy"), P(None, None, "gx", "gy")),
        check_vma=False,
    )
```

time: 576 us -> 93.8 us (0.16)
  blocking collectives: 277 us -> 0 us
  waiting for transfers between devices: 161 us -> 0 us
  Pallas kernels: 0 us -> 85 us
  other arithmetic: 53.6 us -> 0 us
  local copies, waits for them, and re-layouts: 44.2 us -> 7.92 us
  starting transfers between devices: 21.3 us -> 0 us
  between operations: 15.9 us -> 0.67 us
    all_gather x5 -> x0, blocking collectives: 277 us -> none  [carried_in(): everything = jax.tree.map(lambda part: lax.all_gather(part, axis), value)]
    ppermute x8 -> x0, waiting for transfers between devices: 161 us -> none  [the longest x4 161 us: shifted_2(): lax.ppermute(value, axis, [(source, source + steps) for source in range(l...]
    pallas_call x0 -> x1, Pallas kernels: none -> 85 us  [local(): pl.pallas_call(functools.partial(kernel, n, m, nb), out_shape=(jax.ShapeD...]
    transpose x1 -> x0, other arithmetic: 38.2 us -> none  [local(): interpolated.transpose(1, 2, 0, 3, 4)]
    ppermute x8 -> x0, starting transfers between devices: 21.3 us -> none  [the longest x4 10.8 us: shifted_2(): lax.ppermute(value, axis, [(source, source + steps) for source in range(l...]
    slice x18 -> x0, local copies, waits for them, and re-layouts: 14.7 us -> none  [the longest x2 5.48 us: padded_2(): lax.slice_in_dim(block, block.shape[dim] - width, None, axis=dim)]
    unnamed x31 -> x11, local copies, waits for them, and re-layouts: 20.6 us -> 6.11 us
    concatenate x1 -> x0, other arithmetic: 6.04 us -> none  [padded_2(): block = jnp.concatenate([low, block, high], axis=dim)]
  transfers between devices with their start and end apart: 8 -> 0, of which waited for: 2 -> 0; matrix products, arithmetic and copies ran while one was open for 5% -> 0% of each run, Pallas kernels for 0% -> 0%
where the time goes in v1:
time: 93.8 us; the launch traced here: 93.6 us
  Pallas kernels  85 us (91%)
  local copies, waits for them, and re-layouts  7.92 us (8%)
    pallas_call x1, Pallas kernels, local(): pl.pallas_call(functools.partial(kernel, n, m, nb), out_shape=(jax.ShapeD...  85 us
    unnamed x11, local copies, waits for them, and re-layouts  6.11 us

profile of v1, /device:TPU:0, one launch (start us, length us, event | category | flops | bytes accessed | tf_op | source)
XLA Modules:
  0.0 93.6 jit_solution(9116334301617941487)
XLA Ops:
  0.6 0.0 copy-start.2
  0.6 0.9 copy.12.low
  1.5 0.7 copy.13.upp
  2.2 1.8 %copy_bitcast_fusion.1 = (f32[128,8,128]{2,1,0:T(8,128)S(1)}, f32[128,8,128]{2,1,0:T(8,128)S(1)}) fusion(f32[8,128,128]{2,1,0:T(8,128)} %param.9, f32[8,128,128]{2,1,0:T(8,128)} %param.8), kind=kLoop, calls=%fused_computation.1 | loop fusion | bytes 2097152 | tf_op jit(solution)/shard_map/transpose | solution.py:451
  4.1 0.0 copy-done.2
  4.1 0.0 copy-start
  4.1 0.0 copy-start.1
  4.1 2.5 %copy.17 = f32[4,8,128,128]{3,1,0,2:T(8,128)} copy(f32[4,8,128,128]{3,2,1,0:T(8,128)S(1)} %copy-done.2) | data formatting | bytes 4194304 | tf_op args[0]
  6.6 0.0 copy-done
  6.6 0.0 copy-done.1
  6.6 85.0 %shard_map.86 = (f32[2,8,128,128]{3,2,1,0:T(8,128)S(1)}, f32[2,8,128,128]{3,2,1,0:T(8,128)S(1)}) custom-call(s32[64]{0:T(128)S(1)} %bitcast.10, f32[128,4,8,128]{3,2,1,0:T(8,128)} %bitcast.11, f32[128,8,128]{2,1,0:T(8,128)S(1)} %get-tuple-element.3.shx, f32[128,8,128]{2,1,0:T(8,128)S(1)} %get-tuple-element.2.shy, f32[1024,128]{1,0:T(8,128)S(1)} %bitcast.9, ...), custom_call_target="tpu_custom_call" | custom-call | tf_op jit(solution)/shard_map/pallas_call | solution.py:416
  91.6 1.0 %copy.20 = f32[2,8,128,128]{3,2,1,0:T(8,128)} copy(f32[2,8,128,128]{3,2,1,0:T(8,128)S(1)} %get-tuple-element.6) | data formatting | bytes 2097152
  92.6 1.0 %copy.21 = f32[2,8,128,128]{3,2,1,0:T(8,128)} copy(f32[2,8,128,128]{3,2,1,0:T(8,128)S(1)} %get-tuple-element.7) | data formatting | bytes 2097152
Async XLA Ops:
  0.6 3.4 %copy-start.2 = (f32[4,8,128,128]{3,2,1,0:T(8,128)S(1)}, f32[4,8,128,128]{3,2,1,0:T(8,128)}, u32[]{:S(2)}) copy-start(f32[4,8,128,128]{3,2,1,0:T(8,128)} %param.7) | copy-start | bytes 6291460
  4.1 2.6 %copy-start = (f32[8,128,128]{2,1,0:T(8,128)S(1)}, f32[8,128,128]{2,1,0:T(8,128)}, u32[]{:S(2)}) copy-start(f32[8,128,128]{2,1,0:T(8,128)} %param.11) | copy-start | bytes 1572868
  4.1 2.6 %copy-start.1 = (s32[64,1]{0,1:T(1,128)S(1)}, s32[64,1]{0,1:T(1,128)}, u32[]{:S(2)}) copy-start(s32[64,1]{0,1:T(1,128)} %param.10) | copy-start | bytes 772

commit v2 on v1

--- a/solution.py
+++ b/solution.py
@@ -305,19 +305,31 @@
 
     lax.fori_loop(0, n, pivot_step, zero)
 
-    for k in range(CAP):
-        for e, delta in enumerate(DELTA):
-            @pl.when(valid(-delta, 0))
-            def _(e=e, k=k, slot=k * 4 + e):
-                if k == 0:
-                    part_copy(slot, e, 0, BX, slot_s, slot_r, slot).wait_recv()
-                    part_copy(slot, e, BX, 5, rim_s, rim_r, e).wait_recv()
-                else:
-                    part_copy(slot, e, 0, ROWS, slot_s, slot_r, slot).wait_recv()
-        def remote_slot(e, carry, k=k):
-            advect(recv, k * 4 + e)
-            return carry
-        lax.fori_loop(0, 4, remote_slot, 0)
+    def arrive(slot, lo, size, recvs):
+        e = lax.rem(slot, jnp.int32(4))
+        delta = (2 - lax.div(e, jnp.int32(2))) * (1 - 2 * lax.rem(e, jnp.int32(2)))
+
+        @pl.when(valid(-delta, 0))
+        def _():
+            pltpu.make_async_remote_copy(
+                src_ref=send.at[slot, pl.ds(lo, size)], dst_ref=recv.at[slot, pl.ds(lo, size)],
+                send_sem=slot_s.at[slot], recv_sem=recvs.at[slot],
+                device_id=(s + delta, r), device_id_type=MESH,
+            ).wait_recv()
+
+    def first_slot(slot, carry):
+        arrive(slot, 0, BX, slot_r)
+        arrive(slot, BX, 5, rim_r)
+        advect(recv, slot)
+        return carry
+
+    def later_slot(slot, carry):
+        arrive(slot, 0, ROWS, slot_r)
+        advect(recv, slot)
+        return carry
+
+    lax.fori_loop(0, 4, first_slot, 0)
+    lax.fori_loop(4, REMOTE, later_slot, 0)
 
     runs = []
     for i in range(nb):

time: 93.8 us -> 91.4 us (0.974)
  Pallas kernels: 85 us -> 82.6 us
    pallas_call x1, Pallas kernels: 85 us -> 82.6 us  [local(): pl.pallas_call(functools.partial(kernel, n, m, nb), out_shape=(jax.ShapeD...]
where the time goes in v2:
time: 91.4 us; the launch traced here: 91.2 us
  Pallas kernels  82.6 us (90%)
  local copies, waits for them, and re-layouts  7.92 us (9%)
    pallas_call x1, Pallas kernels, local(): pl.pallas_call(functools.partial(kernel, n, m, nb), out_shape=(jax.ShapeD...  82.6 us
    unnamed x11, local copies, waits for them, and re-layouts  6.11 us

profile of v2, /device:TPU:0, one launch (start us, length us, event | category | flops | bytes accessed | tf_op | source)
XLA Modules:
  0.0 91.2 jit_solution(3228485485593357051)
XLA Ops:
  0.6 0.0 copy-start.2
  0.6 0.9 copy.12.low
  1.5 0.7 copy.13.upp
  2.2 1.8 %copy_bitcast_fusion.1 = (f32[128,8,128]{2,1,0:T(8,128)S(1)}, f32[128,8,128]{2,1,0:T(8,128)S(1)}) fusion(f32[8,128,128]{2,1,0:T(8,128)} %param.9, f32[8,128,128]{2,1,0:T(8,128)} %param.8), kind=kLoop, calls=%fused_computation.1 | loop fusion | bytes 2097152 | tf_op jit(solution)/shard_map/transpose | solution.py:463
  4.1 0.0 copy-done.2
  4.1 0.0 copy-start
  4.1 0.0 copy-start.1
  4.1 2.5 %copy.17 = f32[4,8,128,128]{3,1,0,2:T(8,128)} copy(f32[4,8,128,128]{3,2,1,0:T(8,128)S(1)} %copy-done.2) | data formatting | bytes 4194304 | tf_op args[0]
  6.6 0.0 copy-done
  6.6 0.0 copy-done.1
  6.6 82.6 %shard_map.86 = (f32[2,8,128,128]{3,2,1,0:T(8,128)S(1)}, f32[2,8,128,128]{3,2,1,0:T(8,128)S(1)}) custom-call(s32[64]{0:T(128)S(1)} %bitcast.10, f32[128,4,8,128]{3,2,1,0:T(8,128)} %bitcast.11, f32[128,8,128]{2,1,0:T(8,128)S(1)} %get-tuple-element.3.shx, f32[128,8,128]{2,1,0:T(8,128)S(1)} %get-tuple-element.2.shy, f32[1024,128]{1,0:T(8,128)S(1)} %bitcast.9, ...), custom_call_target="tpu_custom_call" | custom-call | tf_op jit(solution)/shard_map/pallas_call | solution.py:428
  89.2 1.0 %copy.20 = f32[2,8,128,128]{3,2,1,0:T(8,128)} copy(f32[2,8,128,128]{3,2,1,0:T(8,128)S(1)} %get-tuple-element.6) | data formatting | bytes 2097152
  90.2 1.0 %copy.21 = f32[2,8,128,128]{3,2,1,0:T(8,128)} copy(f32[2,8,128,128]{3,2,1,0:T(8,128)S(1)} %get-tuple-element.7) | data formatting | bytes 2097152
Async XLA Ops:
  0.6 3.4 %copy-start.2 = (f32[4,8,128,128]{3,2,1,0:T(8,128)S(1)}, f32[4,8,128,128]{3,2,1,0:T(8,128)}, u32[]{:S(2)}) copy-start(f32[4,8,128,128]{3,2,1,0:T(8,128)} %param.7) | copy-start | bytes 6291460
  4.1 2.6 %copy-start = (f32[8,128,128]{2,1,0:T(8,128)S(1)}, f32[8,128,128]{2,1,0:T(8,128)}, u32[]{:S(2)}) copy-start(f32[8,128,128]{2,1,0:T(8,128)} %param.11) | copy-start | bytes 1572868
  4.1 2.6 %copy-start.1 = (s32[64,1]{0,1:T(1,128)S(1)}, s32[64,1]{0,1:T(1,128)}, u32[]{:S(2)}) copy-start(s32[64,1]{0,1:T(1,128)} %param.10) | copy-start | bytes 772

commit v3 on v2

--- a/solution.py
+++ b/solution.py
@@ -80,8 +80,11 @@
 
     lax.fori_loop(0, nb, edges, 0)
 
-    lower = jnp.broadcast_to(low[...], (8, lanes))
-    upper = jnp.broadcast_to(upp[...], (8, lanes))
+    level = lax.broadcasted_iota(jnp.int32, (8, lanes), 0)
+    lower, upper = zero, zero
+    for l in range(levels):
+        lower = jnp.where(level == l, low[l], lower)
+        upper = jnp.where(level == l, upp[l], upper)
     first = jnp.concatenate([ginv[l * cols:l * cols + 1, :] for l in range(levels)], axis=0)
     final = jnp.concatenate([ginv[(l + 1) * cols - 1:(l + 1) * cols, :] for l in range(levels)], axis=0)
     coef[s, 0] = jnp.broadcast_to(first[:, 0:1], (8, lanes)) * lower
@@ -232,11 +235,10 @@
         def spike(x, carry, l=l):
             g = ginv[pl.ds(l * cols + x * 8, 8), :]
             spikes[0, l, pl.ds(x * 8, 8), :] = (
-                jnp.broadcast_to(g[:, 0:1], (8, lanes)) * jnp.broadcast_to(low[l:l + 1, :], (8, lanes))
+                jnp.broadcast_to(g[:, 0:1], (8, lanes)) * low[l]
             )
             spikes[1, l, pl.ds(x * 8, 8), :] = (
-                jnp.broadcast_to(g[:, cols - 1:cols], (8, lanes))
-                * jnp.broadcast_to(upp[l:l + 1, :], (8, lanes))
+                jnp.broadcast_to(g[:, cols - 1:cols], (8, lanes)) * upp[l]
             )
             return carry
         lax.fori_loop(0, cols // 8, spike, 0)
@@ -353,7 +355,7 @@
                 tracers[w, l, pl.ds(i * BX, BX), :] = adv[place, pl.ds(at, BX), :]
             return carry
 
-        lax.fori_loop(0, levels, put, 0)
+        lax.fori_loop(0, levels, put, 0, unroll=4)
 
     def solve(l, carry):
         right = jnp.concatenate([solved[0, l], solved[1, l]], axis=1)
@@ -422,6 +424,7 @@
     nf, levels, cols, lanes = fields.shape
     nb = cols // BX
     vmem = pl.BlockSpec(memory_space=pltpu.VMEM)
+    smem = pl.BlockSpec(memory_space=pltpu.SMEM)
     f32 = jnp.float32
     tile = (8, lanes)
     dma = pltpu.SemaphoreType.DMA
@@ -431,7 +434,7 @@
             jax.ShapeDtypeStruct((2, levels, cols, lanes), f32),
             jax.ShapeDtypeStruct((2, levels, cols, lanes), f32),
         ),
-        in_specs=[pl.BlockSpec(memory_space=pltpu.SMEM)] + [vmem] * 6,
+        in_specs=[smem] + [vmem] * 4 + [smem] * 2,
         out_specs=(vmem, vmem),
         scratch_shapes=[
             pltpu.VMEM((4, nf) + tile, f32),
@@ -462,8 +465,8 @@
         shift_x.transpose(1, 0, 2),
         shift_y.transpose(1, 0, 2),
         group_inverse.reshape(-1, cols),
-        lower,
-        upper,
+        lower[:, 0],
+        upper[:, 0],
     )
 
 

time: 91.4 us -> 89.7 us (0.981)
  local copies, waits for them, and re-layouts: 7.92 us -> 6.5 us
    unnamed x11 -> x13, local copies, waits for them, and re-layouts: 6.11 us -> 4.54 us
where the time goes in v3:
time: 89.7 us; the launch traced here: 89.5 us
  Pallas kernels  82.3 us (92%)
  local copies, waits for them, and re-layouts  6.5 us (7%)
    pallas_call x1, Pallas kernels, local(): pl.pallas_call(functools.partial(kernel, n, m, nb), out_shape=(jax.ShapeD...  82.3 us
    unnamed x13, local copies, waits for them, and re-layouts  4.54 us
    transpose x1, local copies, waits for them, and re-layouts, local(): shift_y.transpose(1, 0, 2)  1.96 us

profile of v3, /device:TPU:0, one launch (start us, length us, event | category | flops | bytes accessed | tf_op | source)
XLA Modules:
  0.0 89.5 jit_solution(8433881553830699741)
XLA Ops:
  0.6 0.0 copy-start.4
  0.6 2.0 %copy_bitcast_fusion.1 = (f32[128,8,128]{2,1,0:T(8,128)S(1)}, f32[128,8,128]{2,1,0:T(8,128)S(1)}) fusion(f32[8,128,128]{2,1,0:T(8,128)} %param.9, f32[8,128,128]{2,1,0:T(8,128)} %param.8), kind=kLoop, calls=%fused_computation.1 | loop fusion | bytes 2097152 | tf_op jit(solution)/shard_map/transpose | solution.py:466
  2.6 0.0 copy-done.4
  2.6 0.0 copy-start
  2.6 0.0 copy-start.1
  2.6 0.0 copy-start.2
  2.6 0.0 copy-start.3
  2.7 2.6 %copy.15 = f32[4,8,128,128]{3,1,0,2:T(8,128)} copy(f32[4,8,128,128]{3,2,1,0:T(8,128)S(1)} %copy-done.4) | data formatting | bytes 4194304 | tf_op args[0]
  5.2 0.0 copy-done
  5.2 0.0 copy-done.1
  5.2 0.0 copy-done.2
  5.2 0.0 copy-done.3
  5.2 82.3 %shard_map.86 = (f32[2,8,128,128]{3,2,1,0:T(8,128)S(1)}, f32[2,8,128,128]{3,2,1,0:T(8,128)S(1)}) custom-call(s32[64]{0:T(128)S(1)} %bitcast.12, f32[128,4,8,128]{3,2,1,0:T(8,128)} %bitcast.15, f32[128,8,128]{2,1,0:T(8,128)S(1)} %get-tuple-element.3.shx, f32[128,8,128]{2,1,0:T(8,128)S(1)} %get-tuple-element.2.shy, f32[1024,128]{1,0:T(8,128)S(1)} %bitcast.11, ...), custom_call_target="tpu_custom_call" | custom-call | tf_op jit(solution)/shard_map/pallas_call | solution.py:431
  87.6 1.0 %copy.18 = f32[2,8,128,128]{3,2,1,0:T(8,128)} copy(f32[2,8,128,128]{3,2,1,0:T(8,128)S(1)} %get-tuple-element.6) | data formatting | bytes 2097152
  88.5 1.0 %copy.19 = f32[2,8,128,128]{3,2,1,0:T(8,128)} copy(f32[2,8,128,128]{3,2,1,0:T(8,128)S(1)} %get-tuple-element.7) | data formatting | bytes 2097152
Async XLA Ops:
  0.6 2.0 %copy-start.4 = (f32[4,8,128,128]{3,2,1,0:T(8,128)S(1)}, f32[4,8,128,128]{3,2,1,0:T(8,128)}, u32[]{:S(2)}) copy-start(f32[4,8,128,128]{3,2,1,0:T(8,128)} %param.7) | copy-start | bytes 6291460
  2.6 2.6 %copy-start = (f32[8,128,128]{2,1,0:T(8,128)S(1)}, f32[8,128,128]{2,1,0:T(8,128)}, u32[]{:S(2)}) copy-start(f32[8,128,128]{2,1,0:T(8,128)} %param.11) | copy-start | bytes 1572868
  2.6 2.6 %copy-start.1 = (s32[64,1]{0,1:T(1,128)S(1)}, s32[64,1]{0,1:T(1,128)}, u32[]{:S(2)}) copy-start(s32[64,1]{0,1:T(1,128)} %param.10) | copy-start | bytes 772
  2.6 2.6 %copy-start.2 = (f32[8,1]{0,1:T(1,128)S(1)}, f32[8,1]{0,1:T(1,128)}, u32[]{:S(2)}) copy-start(f32[8,1]{0,1:T(1,128)} %param.12) | copy-start | bytes 100
  2.6 2.6 %copy-start.3 = (f32[8,1]{0,1:T(1,128)S(1)}, f32[8,1]{0,1:T(1,128)}, u32[]{:S(2)}) copy-start(f32[8,1]{0,1:T(1,128)} %param.13) | copy-start | bytes 100
